TPU v7x, 32 devices: a whole 2x2x4 slice. The times are simulated.
32 devices in a mesh: grp: 2 (over y), blk: 4 (over z), ch: 2 (over x), sub: 2 (over core).
Axes of the slice: x: 2, y: 2, z: 4, core: 2. Of those that a mesh axis runs over, the one named last changes fastest.
Arguments:
- pair_in: bfloat16 [192, 96, 128], P(('grp', 'blk', 'sub'), 'ch'), parts along dimension 0, may hold values from -6 to 6
- cotangent: bfloat16 [192, 96, 128], P(('grp', 'blk', 'sub'), 'ch'), parts along dimension 0, may hold values from -6 to 6
- chain_ids: int32 [192], P('grp'), parts along dimension 0, may hold values from 0 to 3, never falling along the last dimension, each value on 1 to 48 neighbouring positions
- live_length: int32 [2], P('grp'), parts along dimension 0, may hold values from 48 to 96
- chain_embed: float32 [128], replicated, may hold values from -4 to 4
- gain_in: float32 [128], replicated, may hold values from 0.5 to 1.5
- bias_in: float32 [128], replicated, may hold values from -3 to 3
- w_proj: bfloat16 [128, 256], replicated, may hold values from -0.5 to 0.5
- w_gate: bfloat16 [128, 256], replicated, may hold values from -0.5 to 0.5
- w_gout: bfloat16 [128, 128], replicated, may hold values from -0.5 to 0.5
- gain_out: float32 [128], replicated, may hold values from 0.5 to 1.5
- bias_out: float32 [128], replicated, may hold values from -3 to 3
- w_out: bfloat16 [128, 128], replicated, may hold values from -0.5 to 0.5
Outputs:
- new_pair: bfloat16 [192, 96, 128], P(('grp', 'blk', 'sub'), 'ch'), parts along dimension 0
- pair_cols: bfloat16 [192, 96, 128], P(('grp', 'blk', 'sub'), None, 'ch'), parts along dimension 0
- grad_pair: float32 [192, 96, 128], P(('grp', 'blk', 'sub'), 'ch'), parts along dimension 0
- grad_w_proj: float32 [256, 256], P('grp'), parts along dimension 0
- grad_w_gate: float32 [256, 256], P('grp'), parts along dimension 0
- grad_w_gout: float32 [256, 128], P('grp'), parts along dimension 0
- grad_w_out: float32 [256, 128], P('grp'), parts along dimension 0
There are 2 independent parts, one for each index of `grp`. A program takes and returns all parts, laid end to end along the dimension named above; an argument that names none is the same for every part. Nothing has to cross between parts.
All inputs are finite; a program needn't handle non-finite values.
Results may differ from a plain program's by a relative error of at most 0.0061.
Values may be sent and summed in bfloat16 or wider, within the bound.
A program may use at most 64 MiB of HBM per device.

v0:
```python
import jax
import jax.numpy as jnp
from jax import lax
from jax.sharding import PartitionSpec as P

eps = 1e-05


def norm_affine(field, gain, bias):
    mean = jnp.mean(field, axis=-1, keepdims=True)
    centred = field - mean
    spread = jnp.mean(centred * centred, axis=-1, keepdims=True)
    return centred * lax.rsqrt(spread + eps) * gain + bias


def flat_grad(left_cells, right_cells, width_left, width_right):
    left_flat = left_cells.reshape(-1, width_left)
    right_flat = right_cells.reshape(-1, width_right)
    right_high = right_flat.astype(jnp.bfloat16)
    right_low = (right_flat - right_high.astype(jnp.float32)).astype(jnp.bfloat16)
    dims = (((0,), (0,)), ((), ()))
    upper = lax.dot_general(left_flat, right_high, dims, preferred_element_type=jnp.float32)
    lower = lax.dot_general(left_flat, right_low, dims, preferred_element_type=jnp.float32)
    return upper + lower


def fold_right(right_ch, update, initial):
    return update(
        initial, lax.all_gather(right_ch, ("blk", "sub"), axis=0, tiled=True), jnp.int32(0)
    )


def on_device(
    pair_in,
    cotangent,
    chain_ids,
    live_length,
    chain_embed,
    gain_in,
    bias_in,
    w_proj,
    w_gate,
    w_gout,
    gain_out,
    bias_out,
    w_out,
):
    row_count = pair_in.shape[0]
    col_count = pair_in.shape[1]
    width = pair_in.shape[2]
    row_start = lax.axis_index(("blk", "sub")) * row_count
    col_start = lax.axis_index("ch") * col_count
    row_pos = row_start + jnp.arange(row_count, dtype=jnp.int32)
    col_pos = col_start + jnp.arange(col_count, dtype=jnp.int32)
    live_rows = (row_pos < live_length[0]).astype(jnp.float32)
    live_cols = (col_pos < live_length[0]).astype(jnp.float32)
    cell_mask = (live_rows[:, None] * live_cols[None, :])[..., None]
    chain_rows = lax.dynamic_slice_in_dim(chain_ids, row_start, row_count)
    chain_cols = lax.dynamic_slice_in_dim(chain_ids, col_start, col_count)
    same = (chain_rows[:, None] == chain_cols[None, :]).astype(jnp.float32)
    pair = pair_in.astype(jnp.float32) + same[..., None] * chain_embed
    normed, back_in = jax.vjp(lambda field: norm_affine(field, gain_in, bias_in), pair)
    normed_cast = normed.astype(jnp.bfloat16)
    projected = jnp.dot(normed_cast, w_proj, preferred_element_type=jnp.float32)
    gate_pre = jnp.dot(normed_cast, w_gate, preferred_element_type=jnp.float32)
    gout_pre = jnp.dot(normed_cast, w_gout, preferred_element_type=jnp.float32)
    gate_sig = jax.nn.sigmoid(gate_pre)
    gout = jax.nn.sigmoid(gout_pre)
    operands = (projected * gate_sig * cell_mask).astype(jnp.bfloat16)
    left_ch, right_ch = (
        lax.all_to_all(operands[..., :width], "ch", split_axis=2, concat_axis=1, tiled=True),
        lax.all_to_all(operands[..., width:], "ch", split_axis=2, concat_axis=1, tiled=True),
    )

    def add_tri(carry, piece, start):
        update = jnp.einsum("ikc,jkc->ijc", left_ch, piece, preferred_element_type=jnp.float32)
        return update

    tri_sum = fold_right(right_ch, add_tri, jnp.zeros(left_ch.shape, jnp.float32))
    tri_cast = tri_sum.astype(jnp.bfloat16)
    tri_cells = lax.all_to_all(tri_cast, "ch", split_axis=1, concat_axis=2, tiled=True)
    outnorm, back_out = jax.vjp(
        lambda field: norm_affine(field, gain_out, bias_out), tri_cells.astype(jnp.float32)
    )
    outnorm_cast = outnorm.astype(jnp.bfloat16)
    out_lin = jnp.dot(outnorm_cast, w_out, preferred_element_type=jnp.float32)
    new_pair = (pair + out_lin * gout).astype(jnp.bfloat16)
    swapped = lax.all_to_all(
        lax.all_to_all(new_pair, "ch", split_axis=2, concat_axis=1, tiled=True),
        ("blk", "sub"),
        split_axis=1,
        concat_axis=0,
        tiled=True,
    )
    pair_cols = jnp.transpose(swapped, (1, 0, 2))
    d_new = cotangent.astype(jnp.float32)
    d_lin = d_new * gout
    d_gout_pre = d_new * out_lin * gout * (1.0 - gout)
    local_w_out = flat_grad(outnorm_cast, d_lin, width, width)
    d_norm = jnp.dot(d_lin, w_out.astype(jnp.float32).T, precision=lax.Precision.HIGHEST)
    (d_tri,) = back_out(d_norm)
    d_tri_cast = d_tri.astype(jnp.bfloat16)
    d_tri_ch = lax.all_to_all(d_tri_cast, "ch", split_axis=2, concat_axis=1, tiled=True)

    def add_left(carry, piece, start):
        return jnp.einsum("ijc,jkc->ikc", d_tri_ch, piece, preferred_element_type=jnp.float32)

    d_left = fold_right(right_ch, add_left, jnp.zeros(left_ch.shape, jnp.float32))
    d_tri_swap = lax.all_to_all(d_tri_ch, ("blk", "sub"), split_axis=1, concat_axis=0, tiled=True)
    d_right = jnp.einsum(
        "ijc,ikc->jkc",
        d_tri_swap,
        lax.all_gather(left_ch, ("blk", "sub"), axis=0, tiled=True),
        preferred_element_type=jnp.float32,
    )
    back_left, back_right = (
        lax.all_to_all(d_left.astype(jnp.bfloat16), "ch", split_axis=1, concat_axis=2, tiled=True),
        lax.all_to_all(d_right.astype(jnp.bfloat16), "ch", split_axis=1, concat_axis=2, tiled=True),
    )
    d_operands = jnp.concatenate([back_left, back_right], axis=-1).astype(jnp.float32)
    d_proj = d_operands * gate_sig * cell_mask
    d_gate = d_operands * projected * gate_sig * (1.0 - gate_sig) * cell_mask
    local_w_proj = flat_grad(normed_cast, d_proj, width, 2 * width)
    local_w_gate = flat_grad(normed_cast, d_gate, width, 2 * width)
    local_w_gout = flat_grad(normed_cast, d_gout_pre, width, width)
    highest = lax.Precision.HIGHEST
    d_normed = jnp.dot(d_proj, w_proj.astype(jnp.float32).T, precision=highest)
    d_normed = d_normed + jnp.dot(d_gate, w_gate.astype(jnp.float32).T, precision=highest)
    d_normed = d_normed + jnp.dot(d_gout_pre, w_gout.astype(jnp.float32).T, precision=highest)
    (d_pair,) = back_in(d_normed)
    grad_pair = d_new + d_pair
    grad_w_proj, grad_w_gate, grad_w_gout, grad_w_out = lax.psum(
        (local_w_proj, local_w_gate, local_w_gout, local_w_out), ("blk", "ch", "sub")
    )
    return (new_pair, pair_cols, grad_pair, grad_w_proj, grad_w_gate, grad_w_gout, grad_w_out)


def solution(mesh):
    return jax.shard_map(
        on_device,
        mesh=mesh,
        in_specs=(
            P(("grp", "blk", "sub"), "ch", None),
            P(("grp", "blk", "sub"), "ch", None),
            P("grp"),
            P("grp"),
            P(),
            P(),
            P(),
            P(),
            P(),
            P(),
            P(),
            P(),
            P(),
        ),
        out_specs=(
            P(("grp", "blk", "sub"), "ch", None),
            P(("grp", "blk", "sub"), None, "ch"),
            P(("grp", "blk", "sub"), "ch", None),
            P("grp", None),
            P("grp", None),
            P("grp", None),
            P("grp", None),
        ),
        check_vma=False,
    )
```

profile of v0, /device:TPU:0, one launch (start us, length us, event | category | flops | bytes accessed | tf_op | source)
XLA Modules:
  0.0 234.0 jit_solution(18028699892014080564)
XLA Ops:
  7.2 0.7 dynamic_slice.6
  8.0 0.7 dynamic_slice.7
  8.8 1.2 fusion.42
  10.0 1.3 multiply_reduce_fusion.3
  12.1 1.4 fusion.8
  14.5 0.6 reshape.214
  15.1 8.6 %all_to_all.153 = bf16[2,2,18432]{2,1,0:T(2,128)(2,1)S(1)} all-to-all(bf16[2,2,18432]{2,1,0:T(2,128)(2,1)S(1)} %reshape.214), channel_id=1, replica_groups=mesh['grp'=2,'blk'=4,'ch'=2,'sub'=2] {'ch'}, dimensions={0} | all-to-all | bytes 294912 | tf_op jit(solution)/shard_map/all_to_all | solution.py:72
  23.6 0.7 reshape.215
  24.7 0.8 copy.83
  26.0 0.6 reshape.212
  26.6 6.9 %all_to_all.154 = bf16[2,2,18432]{2,1,0:T(2,128)(2,1)S(1)} all-to-all(bf16[2,2,18432]{2,1,0:T(2,128)(2,1)S(1)} %reshape.212), channel_id=1, replica_groups=mesh['grp'=2,'blk'=4,'ch'=2,'sub'=2] {'ch'}, dimensions={0} | all-to-all | bytes 294912 | tf_op jit(solution)/shard_map/all_to_all | solution.py:71
  33.5 0.7 reshape.213
  34.9 16.2 %all-gather.3.cloned.1.call-done = bf16[96,96,64]{1,2,0:T(8,128)(2,1)} async-done(((bf16[12,96,64]{1,2,0:T(8,128)(2,1)}), bf16[96,96,64]{1,2,0:T(8,128)(2,1)}) %all-gather.3.cloned.1.call-update) | async-done | bytes 1179664 | tf_op jit(solution)/shard_map/all_gather | solution.py:29
  51.1 2.7 %fusion.28 = bf16[12,96,64]{1,0,2:T(8,128)(2,1)S(1)} fusion(bf16[12,96,64]{1,0,2:T(8,128)(2,1)S(1)} %copy.87, bf16[96,96,64]{1,2,0:T(8,128)(2,1)} %all-gather.3.cloned.1.call-done), kind=kOutput, calls=%fused_computation.23 | convolution fusion | flops 14229504 | bytes 1474560 | tf_op jit(solution)/shard_map/ikc,jkc->ijc/dot_general | solution.py:76
  53.8 0.5 copy.88
  54.3 0.9 reshape.216
  55.2 3.4 %all-to-all-start.2 = ((bf16[2,2,18432]{2,1,0:T(2,128)(2,1)}), bf16[2,2,18432]{2,1,0:T(2,128)(2,1)S(1)}, u32[]{:S(2)}, u32[]{:S(2)}) async-start(bf16[2,2,18432]{2,1,0:T(2,128)(2,1)} %reshape.216), calls=%async_computation.2 | async-start | bytes 294912 | tf_op jit(solution)/shard_map/all_to_all | solution.py:81
  59.3 0.6 add.138
  60.0 0.6 mul.253
  60.6 0.8 copy.103
  61.5 1.8 all-to-all-done.2
  66.5 1.3 reshape.222
  67.7 4.1 %all-to-all-start.5 = ((bf16[2,2,18432]{2,1,0:T(2,128)(2,1)}), bf16[2,2,18432]{2,1,0:T(2,128)(2,1)}, u32[]{:S(2)}, u32[]{:S(2)}) async-start(bf16[2,2,18432]{2,1,0:T(2,128)(2,1)} %reshape.222), calls=%async_computation.5 | async-start | bytes 294912 | tf_op jit(solution)/shard_map/all_to_all | solution.py:103
  71.8 1.8 subtract_convert_fusion.4
  74.0 1.3 reshape.218
  75.5 0.5 convolution_bitcast_fusion.4
  76.4 4.1 %all-to-all-start.3 = ((bf16[2,2,18432]{2,1,0:T(2,128)(2,1)}), bf16[2,2,18432]{2,1,0:T(2,128)(2,1)}, u32[]{:S(2)}, u32[]{:S(2)}) async-start(bf16[2,2,18432]{2,1,0:T(2,128)(2,1)} %reshape.218), calls=%async_computation.3 | async-start | bytes 294912 | tf_op jit(solution)/shard_map/all_to_all | solution.py:89
  80.5 1.1 fusion.33
  82.0 1.6 reshape.223
  84.0 0.6 copy.118
  84.9 0.9 reshape.224
  85.8 3.4 %all-to-all-start.7 = ((bf16[8,2,4608]{2,1,0:T(2,128)(2,1)}), bf16[8,2,4608]{2,1,0:T(2,128)(2,1)S(1)}, u32[]{:S(2)}, u32[]{:S(2)}) async-start(bf16[8,2,4608]{2,1,0:T(2,128)(2,1)} %reshape.224), calls=%async_computation.7 | async-start | bytes 294912 | tf_op jit(solution)/shard_map/all_to_all | solution.py:109
  89.2 2.7 %fusion.25 = bf16[12,96,64]{1,0,2:T(8,128)(2,1)S(1)} fusion(bf16[12,96,64]{1,0,2:T(8,128)(2,1)S(1)} %copy.99, bf16[96,96,64]{1,2,0:T(8,128)(2,1)} %all-gather.3.cloned.1.call-done), kind=kOutput, calls=%fused_computation.22 | convolution fusion | flops 14229504 | bytes 1474560 | tf_op jit(solution)/shard_map/ijc,jkc->ikc/dot_general | solution.py:106
  92.0 0.5 copy.100
  92.5 0.9 reshape.228
  93.4 2.8 %all-to-all-done.7 = bf16[8,2,4608]{2,1,0:T(2,128)(2,1)S(1)} async-done(((bf16[8,2,4608]{2,1,0:T(2,128)(2,1)}), bf16[8,2,4608]{2,1,0:T(2,128)(2,1)S(1)}, u32[]{:S(2)}, u32[]{:S(2)}) %all-to-all-start.7) | async-done | bytes 147488 | tf_op jit(solution)/shard_map/all_to_all | solution.py:109
  96.2 4.3 %all-to-all-start.6 = ((bf16[2,2,18432]{2,1,0:T(2,128)(2,1)}), bf16[2,2,18432]{2,1,0:T(2,128)(2,1)}, u32[]{:S(2)}, u32[]{:S(2)}) async-start(bf16[2,2,18432]{2,1,0:T(2,128)(2,1)} %reshape.228), calls=%async_computation.6 | async-start | bytes 294912 | tf_op jit(solution)/shard_map/all_to_all | solution.py:117
  100.7 1.6 reshape.219
  102.3 0.6 copy.114
  102.9 0.9 reshape.220
  104.5 0.5 all-to-all-done.6
  105.1 3.4 %all-to-all-start.4 = ((bf16[8,2,4608]{2,1,0:T(2,128)(2,1)}), bf16[8,2,4608]{2,1,0:T(2,128)(2,1)S(1)}, u32[]{:S(2)}, u32[]{:S(2)}) async-start(bf16[8,2,4608]{2,1,0:T(2,128)(2,1)} %reshape.220), calls=%async_computation.4 | async-start | bytes 294912 | tf_op jit(solution)/shard_map/all_to_all | solution.py:88
  108.5 2.7 %fusion.22 = bf16[12,96,64]{1,0,2:T(8,128)(2,1)S(1)} fusion(bf16[96,12,64]{0,1,2:T(8,128)(2,1)S(1)} %copy.108, bf16[96,96,64]{1,2,0:T(8,128)(2,1)} %all-gather.5.cloned.1.call-done), kind=kOutput, calls=%fused_computation.21 | convolution fusion | flops 14229504 | bytes 1474560 | tf_op jit(solution)/shard_map/ijc,ikc->jkc/dot_general | solution.py:110
  111.2 0.5 copy.109
  111.7 0.9 reshape.226
  112.6 2.8 %all-to-all-done.4 = bf16[8,2,4608]{2,1,0:T(2,128)(2,1)S(1)} async-done(((bf16[8,2,4608]{2,1,0:T(2,128)(2,1)}), bf16[8,2,4608]{2,1,0:T(2,128)(2,1)S(1)}, u32[]{:S(2)}, u32[]{:S(2)}) %all-to-all-start.4) | async-done | bytes 147488 | tf_op jit(solution)/shard_map/all_to_all | solution.py:88
  115.4 4.1 %all-to-all-start.8 = ((bf16[2,2,18432]{2,1,0:T(2,128)(2,1)}), bf16[2,2,18432]{2,1,0:T(2,128)(2,1)}, u32[]{:S(2)}, u32[]{:S(2)}) async-start(bf16[2,2,18432]{2,1,0:T(2,128)(2,1)} %reshape.226), calls=%async_computation.8 | async-start | bytes 294912 | tf_op jit(solution)/shard_map/all_to_all | solution.py:118
  119.5 0.9 convolution_add_fusion.2
  120.4 1.2 reshape.229
  122.5 0.8 copy.113
  123.3 0.8 all-to-all-done.8
  124.1 1.2 reshape.227
  125.8 0.6 convolution_bitcast_fusion.2
  126.4 0.5 fusion.58
  127.0 0.5 convolution_bitcast_fusion
  127.5 1.2 fusion.32
  128.7 1.3 fusion.31
  130.8 0.5 fusion.53
  131.3 1.2 convert_add_fusion
  132.5 88.9 %all-reduce.3.cloned.1.call-done = (f32[128,256]{1,0:T(8,128)}, f32[128,256]{1,0:T(8,128)}, f32[128,128]{1,0:T(8,128)}, f32[128,128]{1,0:T(8,128)}) async-done(((f32[128,256]{1,0:T(8,128)}, f32[128,256]{1,0:T(8,128)}, f32[128,128]{1,0:T(8,128)}, f32[128,128]{1,0:T(8,128)}), (f32[128,256]{1,0:T(8,128)}, f32[128,256]{1,0:T(8,128)}, f32[128,128]{1,0:T(8,128)}, ...) | async-done | bytes 393232 | tf_op jit(solution)/shard_map/psum | solution.py:132
  221.4 1.6 copy.145
  223.0 1.6 copy.146
  224.5 1.5 copy.147
  226.0 1.5 copy.148
  (97 shorter events, 11.9 us)
Async XLA Ops:
  7.2 6.3 %copy-start = (bf16[128,256]{1,0:T(8,128)(2,1)S(1)}, bf16[128,256]{1,0:T(8,128)(2,1)}, u32[]{:S(2)}) copy-start(bf16[128,256]{1,0:T(8,128)(2,1)} %param.20) | copy-start | bytes 196612
  7.2 43.9 %all-gather.3.cloned.1.call-start = ((), (), s32[]{:S(2)}) async-start(), calls=%async_computation.9 | async-start | bytes 1769472 | tf_op jit(solution)/shard_map/all_gather | solution.py:29
  11.2 2.3 copy-start.1
  11.3 2.3 copy-start.7
  11.3 2.3 copy-start.10
  11.3 2.3 copy-start.11
  34.9 24.0 %copy-start.8 = (bf16[128,128]{1,0:T(8,128)(2,1)S(1)}, bf16[128,128]{1,0:T(8,128)(2,1)}, u32[]{:S(2)}) copy-start(bf16[128,128]{1,0:T(8,128)(2,1)} %param.22) | copy-start | bytes 98308
  53.8 5.5 %copy-start.18 = (f32[128]{0:T(128)S(1)}, f32[128]{0:T(128)}, u32[]{:S(2)}) copy-start(f32[128]{0:T(128)} %param.24) | copy-start | bytes 1540
  53.8 6.1 %copy-start.14 = (f32[128]{0:T(128)S(1)}, f32[128]{0:T(128)}, u32[]{:S(2)}) copy-start(f32[128]{0:T(128)} %param.23) | copy-start | bytes 1540
  55.2 8.0 %all-to-all-start.2 = ((bf16[2,2,18432]{2,1,0:T(2,128)(2,1)}), bf16[2,2,18432]{2,1,0:T(2,128)(2,1)S(1)}, u32[]{:S(2)}, u32[]{:S(2)}) async-start(bf16[2,2,18432]{2,1,0:T(2,128)(2,1)} %reshape.216), calls=%async_computation.2 | async-start | bytes 294912 | tf_op jit(solution)/shard_map/all_to_all | solution.py:81
  58.6 49.8 %all-gather.5.cloned.1.call-start = ((), (), s32[]{:S(2)}) async-start(), calls=%async_computation.10 | async-start | bytes 1769472 | tf_op jit(solution)/shard_map/all_gather | solution.py:113
  63.7 1.1 copy-start.2
  63.7 1.1 copy-start.5
  63.8 1.1 copy-start.15
  67.7 8.7 %all-to-all-start.5 = ((bf16[2,2,18432]{2,1,0:T(2,128)(2,1)}), bf16[2,2,18432]{2,1,0:T(2,128)(2,1)}, u32[]{:S(2)}, u32[]{:S(2)}) async-start(bf16[2,2,18432]{2,1,0:T(2,128)(2,1)} %reshape.222), calls=%async_computation.5 | async-start | bytes 294912 | tf_op jit(solution)/shard_map/all_to_all | solution.py:103
  71.8 3.5 %copy-start.16 = (f32[2,64]{1,0:T(2,128)S(1)}, f32[2,64]{1,0:T(2,128)}, u32[]{:S(2)}) copy-start(f32[2,64]{1,0:T(2,128)} %add.138) | copy-start | bytes 1540
  71.8 3.5 %copy-start.17 = (f32[2,64]{1,0:T(2,128)S(1)}, f32[2,64]{1,0:T(2,128)}, u32[]{:S(2)}) copy-start(f32[2,64]{1,0:T(2,128)} %mul.253) | copy-start | bytes 1540
  71.8 3.7 %copy-start.12 = (f32[128]{0:T(128)S(1)}, f32[128]{0:T(128)}, u32[]{:S(2)}) copy-start(f32[128]{0:T(128)} %param.19) | copy-start | bytes 1540
  73.6 2.8 %copy-start.4 = (bf16[12,48,128]{2,1,0:T(8,128)(2,1)}, bf16[12,48,128]{2,1,0:T(8,128)(2,1)S(1)}, u32[]{:S(2)}) copy-start(bf16[12,48,128]{2,1,0:T(8,128)(2,1)S(1)} %get-tuple-element.50) | copy-start | bytes 442372
  76.4 9.4 %all-to-all-start.3 = ((bf16[2,2,18432]{2,1,0:T(2,128)(2,1)}), bf16[2,2,18432]{2,1,0:T(2,128)(2,1)}, u32[]{:S(2)}, u32[]{:S(2)}) async-start(bf16[2,2,18432]{2,1,0:T(2,128)(2,1)} %reshape.218), calls=%async_computation.3 | async-start | bytes 294912 | tf_op jit(solution)/shard_map/all_to_all | solution.py:89
  85.8 10.3 %all-to-all-start.7 = ((bf16[8,2,4608]{2,1,0:T(2,128)(2,1)}), bf16[8,2,4608]{2,1,0:T(2,128)(2,1)S(1)}, u32[]{:S(2)}, u32[]{:S(2)}) async-start(bf16[8,2,4608]{2,1,0:T(2,128)(2,1)} %reshape.224), calls=%async_computation.7 | async-start | bytes 294912 | tf_op jit(solution)/shard_map/all_to_all | solution.py:109
  89.2 11.2 %copy-start.3 = (bf16[12,48,128]{2,1,0:T(8,128)(2,1)S(1)}, bf16[12,48,128]{2,1,0:T(8,128)(2,1)}, u32[]{:S(2)}) copy-start(bf16[12,48,128]{2,1,0:T(8,128)(2,1)} %get-tuple-element.35) | copy-start | bytes 442372
  96.2 8.9 %all-to-all-start.6 = ((bf16[2,2,18432]{2,1,0:T(2,128)(2,1)}), bf16[2,2,18432]{2,1,0:T(2,128)(2,1)}, u32[]{:S(2)}, u32[]{:S(2)}) async-start(bf16[2,2,18432]{2,1,0:T(2,128)(2,1)} %reshape.228), calls=%async_computation.6 | async-start | bytes 294912 | tf_op jit(solution)/shard_map/all_to_all | solution.py:117
  105.1 10.3 %all-to-all-start.4 = ((bf16[8,2,4608]{2,1,0:T(2,128)(2,1)}), bf16[8,2,4608]{2,1,0:T(2,128)(2,1)S(1)}, u32[]{:S(2)}, u32[]{:S(2)}) async-start(bf16[8,2,4608]{2,1,0:T(2,128)(2,1)} %reshape.220), calls=%async_computation.4 | async-start | bytes 294912 | tf_op jit(solution)/shard_map/all_to_all | solution.py:88
  115.4 8.7 %all-to-all-start.8 = ((bf16[2,2,18432]{2,1,0:T(2,128)(2,1)}), bf16[2,2,18432]{2,1,0:T(2,128)(2,1)}, u32[]{:S(2)}, u32[]{:S(2)}) async-start(bf16[2,2,18432]{2,1,0:T(2,128)(2,1)} %reshape.226), calls=%async_computation.8 | async-start | bytes 294912 | tf_op jit(solution)/shard_map/all_to_all | solution.py:118
  119.4 101.9 %all-reduce.3.cloned.1.call-start = ((), (), s32[]{:S(2)}) async-start(), calls=%async_computation.11 | async-start | bytes 786432 | tf_op jit(solution)/shard_map/psum | solution.py:132
  122.3 3.4 %copy-start.13 = (f32[128]{0:T(128)S(1)}, f32[128]{0:T(128)}, u32[]{:S(2)}) copy-start(f32[128]{0:T(128)} %param.19) | copy-start | bytes 1540
  127.0 3.0 %copy-start.6 = (bf16[128,256]{1,0:T(8,128)(2,1)S(1)}, bf16[128,256]{1,0:T(8,128)(2,1)}, u32[]{:S(2)}) copy-start(bf16[128,256]{1,0:T(8,128)(2,1)} %param.21) | copy-start | bytes 196612
  128.7 1.7 copy-start.9
Sparse Core Ops, SparseCore 0:
  25.7 25.3 all-gather.2
  61.7 25.0 all-gather.4
  131.5 89.8 all-reduce.2
where the time goes:
time: 235 us; the launch traced here: 234 us
  waiting for transfers between devices  114 us (49%)
  local copies, waits for them, and re-layouts  36 us (15%)
  starting transfers between devices  26.9 us (11%)
  matrix products  20.1 us (9%)
  blocking collectives  15.5 us (7%)
  between operations  15.2 us (6%)
  other arithmetic  5.96 us (3%)
    psum x1, waiting for transfers between devices, on_device(): lax.psum((local_w_proj, local_w_gate, local_w_gout, local_w_out), ('blk',...  88.9 us
    unnamed x61, local copies, waits for them, and re-layouts  22.8 us
    all_gather x1, waiting for transfers between devices, fold_right(): lax.all_gather(right_ch, ('blk', 'sub'), axis=0, tiled=True)  16.2 us
    all_to_all x1, blocking collectives, on_device(): lax.all_to_all(operands[..., width:], 'ch', split_axis=2, concat_axis=1,...  8.57 us
    all_to_all x1, blocking collectives, on_device(): lax.all_to_all(operands[..., :width], 'ch', split_axis=2, concat_axis=1,...  6.91 us
  transfers between devices with their start and end apart: 10, of which 8 were waited for; matrix products, arithmetic and copies ran while one was open for 15% of the time, Pallas kernels for 0%

commit v1 on v0

--- a/solution.py
+++ b/solution.py
@@ -1,6 +1,10 @@
+import functools
+
 import jax
 import jax.numpy as jnp
 from jax import lax
+from jax.experimental import pallas as pl
+from jax.experimental.pallas import tpu as pltpu
 from jax.sharding import PartitionSpec as P
 
 eps = 1e-05
@@ -135,9 +139,501 @@
     return (new_pair, pair_cols, grad_pair, grad_w_proj, grad_w_gate, grad_w_gout, grad_w_out)
 
 
+OPS, TRI, DTRI, DOPS, RS_A, AG_A, RS_B, AG_B, PHASES = range(9)
+
+
+def column_norm(field):
+    mean = jnp.mean(field, axis=0, keepdims=True)
+    centred = field - mean
+    spread = jnp.mean(centred * centred, axis=0, keepdims=True)
+    scale = lax.rsqrt(spread + eps)
+    return centred * scale, scale
+
+
+def column_norm_back(unit, scale, d_unit):
+    first = jnp.mean(d_unit, axis=0, keepdims=True)
+    second = jnp.mean(d_unit * unit, axis=0, keepdims=True)
+    return scale * (d_unit - first - unit * second)
+
+
+def matmul(a, b, dims=((1,), (0,))):
+    return lax.dot_general(a, b, (dims, ((), ())), preferred_element_type=jnp.float32)
+
+
+def low(x):
+    return x.astype(jnp.bfloat16)
+
+
+def wide(x):
+    return x.astype(jnp.float32)
+
+
+def kernel(
+    sizes,
+    rows,
+    cols,
+    live_ref,
+    pair_ref,
+    cot_ref,
+    chain_ref,
+    embed_ref,
+    gain_in_ref,
+    bias_in_ref,
+    gain_out_ref,
+    bias_out_ref,
+    w_proj_ref,
+    w_gate_ref,
+    w_gout_ref,
+    w_out_ref,
+    new_ref,
+    swapped_ref,
+    grad_ref,
+    g_proj_ref,
+    g_gate_ref,
+    g_gout_ref,
+    g_out_ref,
+    s_ops, r_ops, s_tri, r_tri, s_dtri, r_dtri, s_dops, r_dops,
+    s_rsa, r_rsa, s_aga, r_aga, s_rsb, r_rsb, s_agb, r_agb,
+    s_col, r_col,
+    pair_buf, normed_buf, proj_buf, gate_buf, gout_buf, dlin_buf, dnew_buf, dgout_buf,
+    pairs16, pairs8, left_buf, right_buf, flat16, flat8, cells_buf, rows_buf, col_f32, swap_f32,
+    send_sem, recv_sem, col_send, col_recv,
+):
+    nblk, nsub, nch = sizes["blk"], sizes["sub"], sizes["ch"]
+    n = nblk * nsub * nch
+    width = pair_ref.shape[1]
+    per = width // n
+    cells = rows * cols
+    half = cells // 2
+    half_rows = rows // 2
+    tokens = cols * nch
+    my_row = lax.axis_index("blk") * nsub + lax.axis_index("sub")
+    my_ch = lax.axis_index("ch")
+    me = my_row * nch + my_ch
+
+    def place(row, col):
+        return {"blk": row // nsub, "sub": row % nsub, "ch": col}
+
+    def start(phase, src_of, dst):
+        copies = []
+        for t in range(1, n):
+            q = (me + t) % n
+            copy = pltpu.make_async_remote_copy(
+                src_ref=src_of(q),
+                dst_ref=dst.at[me],
+                send_sem=send_sem.at[phase, t],
+                recv_sem=recv_sem.at[phase, t],
+                device_id=place(q // nch, q % nch),
+                device_id_type=pl.DeviceIdType.MESH,
+            )
+            copy.start()
+            copies.append(copy)
+        return copies
+
+    def arrive(phase, copies, dst):
+        for t in range(1, n):
+            q = (me + n - t) % n
+            pltpu.make_async_remote_copy(
+                src_ref=dst.at[q],
+                dst_ref=dst.at[q],
+                send_sem=send_sem.at[phase, t],
+                recv_sem=recv_sem.at[phase, t],
+                device_id=place(q // nch, q % nch),
+                device_id_type=pl.DeviceIdType.MESH,
+            ).wait_recv()
+
+    sent = []
+
+    def exchange(phase, src, dst):
+        sent.extend(start(phase, lambda q: src.at[q], dst))
+        dst[me] = src[me]
+
+    barrier = pltpu.get_barrier_semaphore()
+    for t in range(1, n):
+        q = (me + t) % n
+        pl.semaphore_signal(
+            barrier,
+            inc=1,
+            device_id=place(q // nch, q % nch),
+            device_id_type=pl.DeviceIdType.MESH,
+        )
+
+    vectors = jnp.concatenate(
+        [
+            embed_ref[...],
+            gain_in_ref[...],
+            bias_in_ref[...],
+            gain_out_ref[...],
+            bias_out_ref[...],
+            jnp.zeros((3, width), jnp.float32),
+        ],
+        axis=0,
+    ).T
+    embed, gain_in, bias_in, gain_out, bias_out = [vectors[:, q : q + 1] for q in range(5)]
+
+    cell = lax.broadcasted_iota(jnp.int32, (tokens, cells), 1)
+    token = lax.broadcasted_iota(jnp.int32, (tokens, cells), 0)
+    local_row = jnp.zeros((tokens, cells), jnp.int32)
+    for q in range(1, rows):
+        local_row = local_row + (cell >= q * cols).astype(jnp.int32)
+    row_pos = my_row * rows + local_row
+    col_pos = my_ch * cols + cell - local_row * cols
+    pick = (token == row_pos).astype(jnp.float32) - (token == col_pos).astype(jnp.float32)
+    chain = jnp.broadcast_to(wide(chain_ref[...]), (8, tokens))
+    apart = matmul(low(chain), low(pick))[0:1]
+    same = (apart == 0.0).astype(jnp.float32)
+    length = live_ref[0, 0]
+    mask = (row_pos[0:1] < length).astype(jnp.float32) * (col_pos[0:1] < length).astype(jnp.float32)
+
+    pair = wide(pair_ref[...]).T + same * embed
+    pair_buf[...] = pair
+    unit_in, scale_in = column_norm(pair)
+    normed = low(unit_in * gain_in + bias_in)
+    normed_buf[...] = normed
+    projected = matmul(low(wide(w_proj_ref[...]).T), normed)
+    gate_sig = jax.nn.sigmoid(matmul(low(wide(w_gate_ref[...]).T), normed))
+    masked = gate_sig * mask
+    operands = projected * masked
+    gate_buf[...] = masked
+    proj_buf[...] = operands * (1.0 - gate_sig)
+    for q in range(n):
+        low_q, high_q = q * per, width + q * per
+        s_ops[q] = low(
+            jnp.concatenate(
+                [operands[low_q : low_q + per], operands[high_q : high_q + per]], axis=0
+            )
+        )
+    pl.semaphore_wait(barrier, n - 1)
+    exchange(OPS, s_ops, r_ops)
+
+    gout = jax.nn.sigmoid(matmul(low(wide(w_gout_ref[...]).T), normed))
+    gout_buf[...] = gout
+    d_new = wide(cot_ref[...]).T
+    dnew_buf[...] = d_new
+    d_lin = low(d_new * gout)
+    dlin_buf[...] = d_lin
+    d_unit_out = matmul(w_out_ref[...], d_lin) * gain_out
+    w_out_t = low(wide(w_out_ref[...]).T)
+
+    arrive(OPS, None, r_ops)
+    for q in range(n):
+        block_row, block_col = q // nch, q % nch
+        x = wide(r_ops[q])
+        for i in range(rows):
+            at = (block_row * rows + i) * 2 * per
+            pairs16[at : at + 2 * per, block_col * cols : (block_col + 1) * cols] = x[
+                :, i * cols : (i + 1) * cols
+            ]
+    for c in range(per):
+        left = low(pairs16[pl.ds(c, tokens, stride=2 * per), :])
+        right = low(pairs16[pl.ds(per + c, tokens, stride=2 * per), :])
+        left_buf[c] = left
+        right_buf[c] = right
+        pairs8[pl.ds(c, tokens, stride=per), :] = matmul(left, right, ((1,), (1,)))
+    for q in range(n):
+        block_row, block_col = q // nch, q % nch
+        for i in range(rows):
+            at = (block_row * rows + i) * per
+            down, along = (i // half_rows) * per, (i % half_rows) * cols
+            flat8[q, down : down + per, along : along + cols] = pairs8[
+                at : at + per, block_col * cols : (block_col + 1) * cols
+            ]
+        s_tri[q] = low(flat8[q])
+    exchange(TRI, s_tri, r_tri)
+    arrive(TRI, None, r_tri)
+    for q in range(n):
+        x = wide(r_tri[q])
+        cells_buf[q * per : (q + 1) * per, 0:half] = x[0:per]
+        cells_buf[q * per : (q + 1) * per, half:cells] = x[per : 2 * per]
+
+    unit_out, scale_out = column_norm(cells_buf[...])
+    d_tri = column_norm_back(unit_out, scale_out, d_unit_out)
+    for q in range(n):
+        x = d_tri[q * per : (q + 1) * per]
+        s_dtri[q] = low(jnp.concatenate([x[:, 0:half], x[:, half:cells]], axis=0))
+    exchange(DTRI, s_dtri, r_dtri)
+
+    outnorm = low(unit_out * gain_out + bias_out)
+    out_lin = matmul(w_out_t, outnorm)
+    gout = gout_buf[...]
+    moved = out_lin * gout
+    d_gout = low(dnew_buf[...] * moved * (1.0 - gout))
+    dgout_buf[...] = d_gout
+    grad_gout = matmul(normed_buf[...], d_gout, ((1,), (1,)))
+    grad_out = matmul(outnorm, dlin_buf[...], ((1,), (1,)))
+    for q in range(n):
+        at = q * per
+        s_rsa[q] = low(
+            jnp.concatenate([grad_gout[at : at + per], grad_out[at : at + per]], axis=0)
+        )
+    exchange(RS_A, s_rsa, r_rsa)
+
+    rows_buf[...] = (pair_buf[...] + moved).T
+    new_ref[...] = low(rows_buf[...])
+    share = cols // rows
+    lanes = width // nch
+    first = lax.broadcasted_iota(jnp.int32, (rows, width), 1) < lanes
+    for m in range(share):
+        for j in range(half_rows):
+            a = rows_buf[pl.ds(m * rows + j, rows, stride=cols), :]
+            b = rows_buf[pl.ds(m * rows + j + half_rows, rows, stride=cols), :]
+            col_f32[m * nch, j * rows : (j + 1) * rows, :] = jnp.where(
+                first, a, pltpu.roll(b, lanes, 1)
+            )
+            col_f32[m * nch + 1, j * rows : (j + 1) * rows, :] = jnp.where(
+                first, pltpu.roll(a, lanes, 1), b
+            )
+        for col in range(nch):
+            used = half_rows * rows
+            spare = col_f32.shape[1] - used
+            if spare:
+                col_f32[m * nch + col, used : used + spare, :] = jnp.zeros(
+                    (spare, width), jnp.float32
+                )
+            s_col[m * nch + col] = low(col_f32[m * nch + col])
+
+    def col_copy(slot, row, col):
+        return pltpu.make_async_remote_copy(
+            src_ref=s_col.at[slot],
+            dst_ref=r_col.at[my_row],
+            send_sem=col_send.at[slot],
+            recv_sem=col_recv.at[my_row],
+            device_id=place(row, col),
+            device_id_type=pl.DeviceIdType.MESH,
+        )
+
+    for m in range(share):
+        for col in range(nch):
+            slot = m * nch + col
+            row = my_ch * share + m
+            here = row * nch + col == me
+
+            @pl.when(here)
+            def _():
+                r_col[my_row] = s_col[slot]
+
+            @pl.when(jnp.logical_not(here))
+            def _():
+                col_copy(slot, row, col).start()
+
+    arrive(DTRI, None, r_dtri)
+    for q in range(n):
+        block_row, block_col = q // nch, q % nch
+        x = wide(r_dtri[q])
+        for i in range(rows):
+            at = (block_row * rows + i) * per
+            down, along = (i // half_rows) * per, (i % half_rows) * cols
+            pairs8[at : at + per, block_col * cols : (block_col + 1) * cols] = x[
+                down : down + per, along : along + cols
+            ]
+    for c in range(per):
+        grad = pairs8[pl.ds(c, tokens, stride=per), :]
+        pairs16[pl.ds(c, tokens, stride=2 * per), :] = matmul(low(grad), right_buf[c])
+        pairs16[pl.ds(per + c, tokens, stride=2 * per), :] = matmul(low(grad.T), left_buf[c])
+    for q in range(n):
+        block_row, block_col = q // nch, q % nch
+        for i in range(rows):
+            at = (block_row * rows + i) * 2 * per
+            flat16[q, :, i * cols : (i + 1) * cols] = pairs16[
+                at : at + 2 * per, block_col * cols : (block_col + 1) * cols
+            ]
+        s_dops[q] = low(flat16[q])
+    exchange(DOPS, s_dops, r_dops)
+
+    def summed(buf):
+        total = wide(buf[0])
+        for q in range(1, n):
+            total = total + wide(buf[q])
+        return low(total)
+
+    arrive(RS_A, None, r_rsa)
+    s_aga[...] = summed(r_rsa)
+    sent.extend(start(AG_A, lambda q: s_aga, r_aga))
+    r_aga[me] = s_aga[...]
+
+    for row in range(nblk * nsub):
+        source = row * nch + my_row // share
+
+        @pl.when(source != me)
+        def _():
+            pltpu.make_async_remote_copy(
+                src_ref=r_col.at[row],
+                dst_ref=r_col.at[row],
+                send_sem=col_send.at[0],
+                recv_sem=col_recv.at[row],
+                device_id=place(row, my_row // share),
+                device_id_type=pl.DeviceIdType.MESH,
+            ).wait_recv()
+
+        for j in range(half_rows):
+            x = wide(r_col[row])[j * rows : (j + 1) * rows]
+            swap_f32[j, row * rows : (row + 1) * rows, :] = x[:, 0:lanes]
+            swap_f32[j + half_rows, row * rows : (row + 1) * rows, :] = x[:, lanes:width]
+    swapped_ref[...] = low(swap_f32[...])
+    d_normed_gout = matmul(w_gout_ref[...], dgout_buf[...])
+
+    arrive(DOPS, None, r_dops)
+    d_operands = jnp.concatenate(
+        [wide(r_dops[q])[0:per] for q in range(n)]
+        + [wide(r_dops[q])[per : 2 * per] for q in range(n)],
+        axis=0,
+    )
+    d_proj = low(d_operands * gate_buf[...])
+    d_gate = low(d_operands * proj_buf[...])
+    normed = normed_buf[...]
+    grad_proj = matmul(normed, d_proj, ((1,), (1,)))
+    grad_gate = matmul(normed, d_gate, ((1,), (1,)))
+    for q in range(n):
+        at = q * per
+        s_rsb[q] = low(
+            jnp.concatenate([grad_proj[at : at + per], grad_gate[at : at + per]], axis=0)
+        )
+    exchange(RS_B, s_rsb, r_rsb)
+
+    d_normed = d_normed_gout + matmul(w_proj_ref[...], d_proj) + matmul(w_gate_ref[...], d_gate)
+    unit_in, scale_in = column_norm(pair_buf[...])
+    d_pair = column_norm_back(unit_in, scale_in, d_normed * gain_in)
+    total = dnew_buf[...] + d_pair
+
+    arrive(RS_B, None, r_rsb)
+    s_agb[...] = summed(r_rsb)
+    sent.extend(start(AG_B, lambda q: s_agb, r_agb))
+    r_agb[me] = s_agb[...]
+    grad_ref[...] = total.T
+    arrive(AG_A, None, r_aga)
+    for q in range(n):
+        x = wide(r_aga[q])
+        g_gout_ref[q * per : (q + 1) * per, :] = x[0:per]
+        g_out_ref[q * per : (q + 1) * per, :] = x[per : 2 * per]
+    arrive(AG_B, None, r_agb)
+    for q in range(n):
+        x = wide(r_agb[q])
+        g_proj_ref[q * per : (q + 1) * per, :] = x[0:per]
+        g_gate_ref[q * per : (q + 1) * per, :] = x[per : 2 * per]
+
+    for copy in sent:
+        copy.wait_send()
+    for m in range(share):
+        for col in range(nch):
+            slot = m * nch + col
+            row = my_ch * share + m
+
+            @pl.when(row * nch + col != me)
+            def _():
+                col_copy(slot, row, col).wait_send()
+
+
+def fused(
+    sizes,
+    pair_in,
+    cotangent,
+    chain_ids,
+    live_length,
+    chain_embed,
+    gain_in,
+    bias_in,
+    w_proj,
+    w_gate,
+    w_gout,
+    gain_out,
+    bias_out,
+    w_out,
+):
+    rows, cols, width = pair_in.shape
+    n = sizes["blk"] * sizes["sub"] * sizes["ch"]
+    per = width // n
+    cells, tokens, lanes = rows * cols, cols * sizes["ch"], width // sizes["ch"]
+    half = cells // 2
+    slots = cols // rows * sizes["ch"]
+    col_rows = -(-(rows // 2 * rows) // 16) * 16
+    bf, f32 = jnp.bfloat16, jnp.float32
+    vm = pltpu.VMEM
+
+    def both(*shape):
+        return [vm((n,) + shape, bf), vm((n,) + shape, bf)]
+
+    line = lambda x: x.reshape(1, -1)
+    outs = pl.pallas_call(
+        functools.partial(kernel, sizes, rows, cols),
+        out_shape=(
+            jax.ShapeDtypeStruct((cells, width), bf),
+            jax.ShapeDtypeStruct((rows, tokens, lanes), bf),
+            jax.ShapeDtypeStruct((cells, width), f32),
+            jax.ShapeDtypeStruct((width, 2 * width), f32),
+            jax.ShapeDtypeStruct((width, 2 * width), f32),
+            jax.ShapeDtypeStruct((width, width), f32),
+            jax.ShapeDtypeStruct((width, width), f32),
+        ),
+        in_specs=[pl.BlockSpec(memory_space=pltpu.SMEM)]
+        + [pl.BlockSpec(memory_space=pltpu.VMEM)] * 12,
+        out_specs=[pl.BlockSpec(memory_space=pltpu.VMEM)] * 7,
+        scratch_shapes=both(2 * per, cells)
+        + both(2 * per, half)
+        + both(2 * per, half)
+        + both(2 * per, cells)
+        + both(2 * per, width)
+        + [vm((2 * per, width), bf), vm((n, 2 * per, width), bf)]
+        + both(2 * per, 2 * width)
+        + [vm((2 * per, 2 * width), bf), vm((n, 2 * per, 2 * width), bf)]
+        + [vm((slots, col_rows, width), bf), vm((n // sizes["ch"], col_rows, width), bf)]
+        + [
+            vm((width, cells), f32),
+            vm((width, cells), bf),
+            vm((2 * width, cells), f32),
+            vm((2 * width, cells), f32),
+            vm((width, cells), f32),
+            vm((width, cells), bf),
+            vm((width, cells), f32),
+            vm((width, cells), bf),
+            vm((tokens * 2 * per, tokens), f32),
+            vm((tokens * per, tokens), f32),
+            vm((per, tokens, tokens), bf),
+            vm((per, tokens, tokens), bf),
+            vm((n, 2 * per, cells), f32),
+            vm((n, 2 * per, half), f32),
+            vm((width, cells), f32),
+            vm((cells, width), f32),
+            vm((slots, col_rows, width), f32),
+            vm((rows, tokens, lanes), f32),
+            pltpu.SemaphoreType.DMA((PHASES, n)),
+            pltpu.SemaphoreType.DMA((PHASES, n)),
+            pltpu.SemaphoreType.DMA((slots,)),
+            pltpu.SemaphoreType.DMA((n // sizes["ch"],)),
+        ],
+        compiler_params=pltpu.CompilerParams(
+            collective_id=0, has_side_effects=True, vmem_limit_bytes=40 << 20
+        ),
+    )(
+        line(live_length),
+        pair_in.reshape(cells, width),
+        cotangent.reshape(cells, width),
+        line(chain_ids),
+        line(chain_embed),
+        line(gain_in),
+        line(bias_in),
+        line(gain_out),
+        line(bias_out),
+        w_proj,
+        w_gate,
+        w_gout,
+        w_out,
+    )
+    new_pair, pair_cols, grad_pair, *grads = outs
+    return (
+        new_pair.reshape(rows, cols, width),
+        pair_cols,
+        grad_pair.reshape(rows, cols, width),
+        *grads,
+    )
+
+
 def solution(mesh):
+    sizes = dict(mesh.shape)
+    devices = sizes["blk"] * sizes["sub"] * sizes["ch"]
+    fits = devices * 8 == 128 and sizes["ch"] == 2
+    body = functools.partial(fused, sizes) if fits else on_device
     return jax.shard_map(
-        on_device,
+        body,
         mesh=mesh,
         in_specs=(
             P(("grp", "blk", "sub"), "ch", None),

time: 235 us -> 68.6 us (0.29)
  waiting for transfers between devices: 114 us -> 0 us
  Pallas kernels: 0 us -> 56.4 us
  starting transfers between devices: 26.9 us -> 0 us
  local copies, waits for them, and re-layouts: 36 us -> 10.5 us
  matrix products: 20.1 us -> 0 us
  blocking collectives: 15.5 us -> 0 us
  between operations: 15.2 us -> 1.35 us
  other arithmetic: 5.96 us -> 0 us
    psum x1 -> x0, waiting for transfers between devices: 88.9 us -> none  [on_device(): lax.psum((local_w_proj, local_w_gate, local_w_gout, local_w_out), ('blk',...]
    pallas_call x0 -> x1, Pallas kernels: none -> 56.4 us  [fused(): pl.pallas_call(functools.partial(kernel, sizes, rows, cols), out_shape=(j...]
    all_to_all x7 -> x0, starting transfers between devices: 26.6 us -> none  [the longest x1 4.27 us: on_device(): lax.all_to_all(d_left.astype(jnp.bfloat16), 'ch', split_axis=1, concat_ax...]
    dot_general x19 -> x0, matrix products: 20.1 us -> none  [the longest x4 3.83 us: flat_grad(): lax.dot_general(left_flat, right_high, dims, preferred_element_type=jnp.f...]
    all_gather x2 -> x0, waiting for transfers between devices: 16.2 us -> none  [the longest x1 16.2 us: fold_right(): lax.all_gather(right_ch, ('blk', 'sub'), axis=0, tiled=True)]
    all_to_all x2 -> x0, blocking collectives: 15.5 us -> none  [the longest x1 8.57 us: on_device(): lax.all_to_all(operands[..., width:], 'ch', split_axis=2, concat_axis=1,...]
    unnamed x61 -> x31, local copies, waits for them, and re-layouts: 22.8 us -> 10.5 us
    all_to_all x7 -> x0, waiting for transfers between devices: 9.13 us -> none  [the longest x1 2.83 us: on_device(): lax.all_to_all(lax.all_to_all(new_pair, 'ch', split_axis=2, concat_axis=1...]
  transfers between devices with their start and end apart: 10 -> 0, of which waited for: 8 -> 0; matrix products, arithmetic and copies ran while one was open for 15% -> 0% of each run, Pallas kernels for 0% -> 0%
where the time goes in v1:
time: 68.6 us; the launch traced here: 68.2 us
  Pallas kernels  56.4 us (82%)
  local copies, waits for them, and re-layouts  10.5 us (15%)
  between operations  1.35 us (2%)
    pallas_call x1, Pallas kernels, fused(): pl.pallas_call(functools.partial(kernel, sizes, rows, cols), out_shape=(j...  56.4 us
    unnamed x31, local copies, waits for them, and re-layouts  10.5 us

profile of v1, /device:TPU:0, one launch (start us, length us, event | category | flops | bytes accessed | tf_op | source)
XLA Modules:
  0.0 68.2 jit_solution(15388275274113168971)
XLA Ops:
  1.3 0.0 copy-start.9
  1.3 0.0 copy-start.10
  1.3 0.0 copy-start.11
  1.3 0.0 copy-start.6
  1.3 0.0 copy-start.7
  1.3 0.0 copy-start.8
  1.3 0.6 copy-done.9
  1.9 0.0 copy-done.10
  2.0 0.0 copy-done.11
  2.0 0.0 copy-done.6
  2.0 0.0 copy-done.7
  2.0 0.0 copy-done.8
  2.0 0.0 copy-start
  2.0 0.9 %copy-done = bf16[12,48,128]{2,1,0:T(8,128)(2,1)S(1)} copy-done((bf16[12,48,128]{2,1,0:T(8,128)(2,1)S(1)}, bf16[12,48,128]{2,1,0:T(8,128)(2,1)}, u32[]{:S(2)}) %copy-start) | copy-done | bytes 147480
  2.9 0.0 copy-start.1
  2.9 0.9 %copy-done.1 = bf16[12,48,128]{2,1,0:T(8,128)(2,1)S(1)} copy-done((bf16[12,48,128]{2,1,0:T(8,128)(2,1)S(1)}, bf16[12,48,128]{2,1,0:T(8,128)(2,1)}, u32[]{:S(2)}) %copy-start.1) | copy-done | bytes 147480
  3.8 0.0 copy-start.2
  3.8 0.8 %copy-done.2 = bf16[128,256]{1,0:T(8,128)(2,1)S(1)} copy-done((bf16[128,256]{1,0:T(8,128)(2,1)S(1)}, bf16[128,256]{1,0:T(8,128)(2,1)}, u32[]{:S(2)}) %copy-start.2) | copy-done | bytes 65560
  4.7 0.0 copy-start.3
  4.7 0.8 %copy-done.3 = bf16[128,256]{1,0:T(8,128)(2,1)S(1)} copy-done((bf16[128,256]{1,0:T(8,128)(2,1)S(1)}, bf16[128,256]{1,0:T(8,128)(2,1)}, u32[]{:S(2)}) %copy-start.3) | copy-done | bytes 65560
  5.5 0.0 copy-start.4
  5.5 0.8 %copy-done.4 = bf16[128,128]{1,0:T(8,128)(2,1)S(1)} copy-done((bf16[128,128]{1,0:T(8,128)(2,1)S(1)}, bf16[128,128]{1,0:T(8,128)(2,1)}, u32[]{:S(2)}) %copy-start.4) | copy-done | bytes 32792
  6.3 0.0 copy-start.5
  6.3 0.8 %copy-done.5 = bf16[128,128]{1,0:T(8,128)(2,1)S(1)} copy-done((bf16[128,128]{1,0:T(8,128)(2,1)S(1)}, bf16[128,128]{1,0:T(8,128)(2,1)}, u32[]{:S(2)}) %copy-start.5) | copy-done | bytes 32792
  7.0 56.4 %shard_map.180 = (bf16[576,128]{1,0:T(8,128)(2,1)S(1)}, bf16[12,96,64]{2,1,0:T(8,128)(2,1)S(1)}, f32[576,128]{1,0:T(8,128)S(1)}, f32[128,256]{1,0:T(8,128)S(1)},...) custom-call(s32[1,1]{1,0:T(1,128)} %bitcast.11.live_ref, bf16[576,128]{1,0:T(8,128)(2,1)S(1)} %bitcast.13, ...), custom_call_target="tpu_custom_call" | custom-call | tf_op jit(solution)/shard_map/pallas_call | solution.py:556
  63.5 0.8 %copy.20 = bf16[12,96,64]{1,2,0:T(8,128)(2,1)} copy(bf16[12,96,64]{2,1,0:T(8,128)(2,1)S(1)} %get-tuple-element.22) | data formatting | bytes 294912
  64.3 0.7 copy.28
  64.9 0.7 %copy.29 = f32[12,48,128]{2,1,0:T(8,128)} copy(f32[12,48,128]{2,1,0:T(8,128)S(1)} %bitcast.12) | data formatting | bytes 589824
  65.7 0.7 copy.30
  66.3 0.7 copy.31
  67.0 0.6 copy.32
  67.6 0.6 copy.33
Async XLA Ops:
  1.3 0.7 copy-start.9
  1.3 0.7 copy-start.10
  1.3 0.7 copy-start.11
  1.3 0.7 copy-start.6
  1.3 0.7 copy-start.7
  1.3 0.7 %copy-start.8 = (f32[128]{0:T(128)S(1)}, f32[128]{0:T(128)}, u32[]{:S(2)}) copy-start(f32[128]{0:T(128)} %param.18) | copy-start | bytes 1540
  2.0 0.9 %copy-start = (bf16[12,48,128]{2,1,0:T(8,128)(2,1)S(1)}, bf16[12,48,128]{2,1,0:T(8,128)(2,1)}, u32[]{:S(2)}) copy-start(bf16[12,48,128]{2,1,0:T(8,128)(2,1)} %param.13) | copy-start | bytes 442372
  2.9 0.9 %copy-start.1 = (bf16[12,48,128]{2,1,0:T(8,128)(2,1)S(1)}, bf16[12,48,128]{2,1,0:T(8,128)(2,1)}, u32[]{:S(2)}) copy-start(bf16[12,48,128]{2,1,0:T(8,128)(2,1)} %param.14) | copy-start | bytes 442372
  3.8 0.8 %copy-start.2 = (bf16[128,256]{1,0:T(8,128)(2,1)S(1)}, bf16[128,256]{1,0:T(8,128)(2,1)}, u32[]{:S(2)}) copy-start(bf16[128,256]{1,0:T(8,128)(2,1)} %w_proj_ref.1) | copy-start | bytes 196612
  4.7 0.8 %copy-start.3 = (bf16[128,256]{1,0:T(8,128)(2,1)S(1)}, bf16[128,256]{1,0:T(8,128)(2,1)}, u32[]{:S(2)}) copy-start(bf16[128,256]{1,0:T(8,128)(2,1)} %w_gate_ref.1) | copy-start | bytes 196612
  5.5 0.8 %copy-start.4 = (bf16[128,128]{1,0:T(8,128)(2,1)S(1)}, bf16[128,128]{1,0:T(8,128)(2,1)}, u32[]{:S(2)}) copy-start(bf16[128,128]{1,0:T(8,128)(2,1)} %w_gout_ref.1) | copy-start | bytes 98308
  6.3 0.8 %copy-start.5 = (bf16[128,128]{1,0:T(8,128)(2,1)S(1)}, bf16[128,128]{1,0:T(8,128)(2,1)}, u32[]{:S(2)}) copy-start(bf16[128,128]{1,0:T(8,128)(2,1)} %w_out_ref.1) | copy-start | bytes 98308

commit v2 on v1

--- a/solution.py
+++ b/solution.py
@@ -139,6 +139,8 @@
     return (new_pair, pair_cols, grad_pair, grad_w_proj, grad_w_gate, grad_w_gout, grad_w_out)
 
 
+most_vmem = (64 << 20) - (96 << 10)
+
 OPS, TRI, DTRI, DOPS, RS_A, AG_A, RS_B, AG_B, PHASES = range(9)
 
 
@@ -173,6 +175,11 @@
     rows,
     cols,
     live_ref,
+    *refs,
+):
+    inputs, outputs, scratch = refs[:12], refs[12:19], refs[19:]
+    loaded, made, scratch = scratch[:12], scratch[12:19], scratch[19:]
+    (
     pair_ref,
     cot_ref,
     chain_ref,
@@ -185,6 +192,8 @@
     w_gate_ref,
     w_gout_ref,
     w_out_ref,
+    ) = loaded
+    (
     new_ref,
     swapped_ref,
     grad_ref,
@@ -192,13 +201,15 @@
     g_gate_ref,
     g_gout_ref,
     g_out_ref,
+    ) = made
+    (
     s_ops, r_ops, s_tri, r_tri, s_dtri, r_dtri, s_dops, r_dops,
     s_rsa, r_rsa, s_aga, r_aga, s_rsb, r_rsb, s_agb, r_agb,
     s_col, r_col,
     pair_buf, normed_buf, proj_buf, gate_buf, gout_buf, dlin_buf, dnew_buf, dgout_buf,
     pairs16, pairs8, left_buf, right_buf, flat16, flat8, cells_buf, rows_buf, col_f32, swap_f32,
-    send_sem, recv_sem, col_send, col_recv,
-):
+    send_sem, recv_sem, col_send, col_recv, load_sem, store_sem,
+    ) = scratch
     nblk, nsub, nch = sizes["blk"], sizes["sub"], sizes["ch"]
     n = nblk * nsub * nch
     width = pair_ref.shape[1]
@@ -214,10 +225,18 @@
     def place(row, col):
         return {"blk": row // nsub, "sub": row % nsub, "ch": col}
 
+    def partner(t):
+        q, bit = me, 1
+        while bit <= t:
+            if t & bit:
+                q = q + bit * (1 - 2 * (me // bit % 2))
+            bit *= 2
+        return q
+
     def start(phase, src_of, dst):
         copies = []
-        for t in range(1, n):
-            q = (me + t) % n
+        for t in reversed(range(1, n)):
+            q = partner(t)
             copy = pltpu.make_async_remote_copy(
                 src_ref=src_of(q),
                 dst_ref=dst.at[me],
@@ -232,7 +251,7 @@
 
     def arrive(phase, copies, dst):
         for t in range(1, n):
-            q = (me + n - t) % n
+            q = partner(t)
             pltpu.make_async_remote_copy(
                 src_ref=dst.at[q],
                 dst_ref=dst.at[q],
@@ -244,19 +263,30 @@
 
     sent = []
 
+    def store(q):
+        pltpu.make_async_copy(made[q], outputs[q], store_sem.at[q]).start()
+
     def exchange(phase, src, dst):
         sent.extend(start(phase, lambda q: src.at[q], dst))
         dst[me] = src[me]
 
     barrier = pltpu.get_barrier_semaphore()
     for t in range(1, n):
-        q = (me + t) % n
+        q = partner(t)
         pl.semaphore_signal(
             barrier,
             inc=1,
             device_id=place(q // nch, q % nch),
             device_id_type=pl.DeviceIdType.MESH,
         )
+
+    loads = [
+        pltpu.make_async_copy(inputs[q], loaded[q], load_sem.at[q]) for q in range(12)
+    ]
+    for load in loads:
+        load.start()
+    for load in loads:
+        load.wait()
 
     vectors = jnp.concatenate(
         [
@@ -370,6 +400,7 @@
 
     rows_buf[...] = (pair_buf[...] + moved).T
     new_ref[...] = low(rows_buf[...])
+    store(0)
     share = cols // rows
     lanes = width // nch
     first = lax.broadcasted_iota(jnp.int32, (rows, width), 1) < lanes
@@ -469,7 +500,9 @@
             x = wide(r_col[row])[j * rows : (j + 1) * rows]
             swap_f32[j, row * rows : (row + 1) * rows, :] = x[:, 0:lanes]
             swap_f32[j + half_rows, row * rows : (row + 1) * rows, :] = x[:, lanes:width]
-    swapped_ref[...] = low(swap_f32[...])
+    for j in range(rows):
+        swapped_ref[j] = low(swap_f32[j].T)
+    store(1)
     d_normed_gout = matmul(w_gout_ref[...], dgout_buf[...])
 
     arrive(DOPS, None, r_dops)
@@ -500,17 +533,22 @@
     sent.extend(start(AG_B, lambda q: s_agb, r_agb))
     r_agb[me] = s_agb[...]
     grad_ref[...] = total.T
+    store(2)
     arrive(AG_A, None, r_aga)
     for q in range(n):
         x = wide(r_aga[q])
         g_gout_ref[q * per : (q + 1) * per, :] = x[0:per]
         g_out_ref[q * per : (q + 1) * per, :] = x[per : 2 * per]
+    store(5)
+    store(6)
     arrive(AG_B, None, r_agb)
     for q in range(n):
         x = wide(r_agb[q])
         g_proj_ref[q * per : (q + 1) * per, :] = x[0:per]
         g_gate_ref[q * per : (q + 1) * per, :] = x[per : 2 * per]
 
+    store(3)
+    store(4)
     for copy in sent:
         copy.wait_send()
     for m in range(share):
@@ -521,6 +559,31 @@
             @pl.when(row * nch + col != me)
             def _():
                 col_copy(slot, row, col).wait_send()
+
+    for q in range(7):
+        pltpu.make_async_copy(made[q], outputs[q], store_sem.at[q]).wait()
+
+
+def write_kernel(*refs):
+    count = len(refs) // 2
+    copies = [
+        pltpu.make_async_copy(refs[q], refs[count + q], refs[-1].at[q]) for q in range(count)
+    ]
+    for copy in copies:
+        copy.start()
+    for copy in copies:
+        copy.wait()
+
+
+def write_out(values):
+    return pl.pallas_call(
+        write_kernel,
+        out_shape=tuple(jax.ShapeDtypeStruct(x.shape, x.dtype) for x in values),
+        in_specs=[pl.BlockSpec(memory_space=pltpu.HBM)] * len(values),
+        out_specs=[pl.BlockSpec(memory_space=pltpu.HBM)] * len(values),
+        scratch_shapes=[pltpu.SemaphoreType.DMA((len(values),))],
+        compiler_params=pltpu.CompilerParams(vmem_limit_bytes=most_vmem),
+    )(*values)
 
 
 def fused(
@@ -553,21 +616,37 @@
         return [vm((n,) + shape, bf), vm((n,) + shape, bf)]
 
     line = lambda x: x.reshape(1, -1)
+    operands = (
+        pair_in.reshape(cells, width),
+        cotangent.reshape(cells, width),
+        line(chain_ids),
+        line(chain_embed),
+        line(gain_in),
+        line(bias_in),
+        line(gain_out),
+        line(bias_out),
+        w_proj,
+        w_gate,
+        w_gout,
+        w_out,
+    )
+    results = (
+        jax.ShapeDtypeStruct((cells, width), bf),
+        jax.ShapeDtypeStruct((rows, lanes, tokens), bf),
+        jax.ShapeDtypeStruct((cells, width), f32),
+        jax.ShapeDtypeStruct((width, 2 * width), f32),
+        jax.ShapeDtypeStruct((width, 2 * width), f32),
+        jax.ShapeDtypeStruct((width, width), f32),
+        jax.ShapeDtypeStruct((width, width), f32),
+    )
     outs = pl.pallas_call(
         functools.partial(kernel, sizes, rows, cols),
-        out_shape=(
-            jax.ShapeDtypeStruct((cells, width), bf),
-            jax.ShapeDtypeStruct((rows, tokens, lanes), bf),
-            jax.ShapeDtypeStruct((cells, width), f32),
-            jax.ShapeDtypeStruct((width, 2 * width), f32),
-            jax.ShapeDtypeStruct((width, 2 * width), f32),
-            jax.ShapeDtypeStruct((width, width), f32),
-            jax.ShapeDtypeStruct((width, width), f32),
-        ),
+        out_shape=results,
         in_specs=[pl.BlockSpec(memory_space=pltpu.SMEM)]
-        + [pl.BlockSpec(memory_space=pltpu.VMEM)] * 12,
-        out_specs=[pl.BlockSpec(memory_space=pltpu.VMEM)] * 7,
-        scratch_shapes=both(2 * per, cells)
+        + [pl.BlockSpec(memory_space=pltpu.HBM)] * 12,
+        out_specs=[pl.BlockSpec(memory_space=pltpu.HBM)] * 7,
+        scratch_shapes=[vm(x.shape, x.dtype) for x in operands + results]
+        + both(2 * per, cells)
         + both(2 * per, half)
         + both(2 * per, half)
         + both(2 * per, cells)
@@ -599,29 +678,18 @@
             pltpu.SemaphoreType.DMA((PHASES, n)),
             pltpu.SemaphoreType.DMA((slots,)),
             pltpu.SemaphoreType.DMA((n // sizes["ch"],)),
+            pltpu.SemaphoreType.DMA((12,)),
+            pltpu.SemaphoreType.DMA((7,)),
         ],
         compiler_params=pltpu.CompilerParams(
-            collective_id=0, has_side_effects=True, vmem_limit_bytes=40 << 20
+            collective_id=0, has_side_effects=True, vmem_limit_bytes=most_vmem
         ),
-    )(
-        line(live_length),
-        pair_in.reshape(cells, width),
-        cotangent.reshape(cells, width),
-        line(chain_ids),
-        line(chain_embed),
-        line(gain_in),
-        line(bias_in),
-        line(gain_out),
-        line(bias_out),
-        w_proj,
-        w_gate,
-        w_gout,
-        w_out,
-    )
+    )(line(live_length), *operands)
+    outs = write_out(outs)
     new_pair, pair_cols, grad_pair, *grads = outs
     return (
         new_pair.reshape(rows, cols, width),
-        pair_cols,
+        jnp.swapaxes(pair_cols, 1, 2),
         grad_pair.reshape(rows, cols, width),
         *grads,
     )

time: 68.6 us -> 91 us (1.33)
  Pallas kernels: 56.4 us -> 89.6 us
  local copies, waits for them, and re-layouts: 10.5 us -> 0 us
    pallas_call x1 -> x2, Pallas kernels: 56.4 us -> 89.6 us  [the longest x1 57.1 us: fused(): pl.pallas_call(functools.partial(kernel, sizes, rows, cols), out_shape=re...]
    unnamed x31 -> x0, local copies, waits for them, and re-layouts: 10.5 us -> none
where the time goes in v2:
time: 91 us; the launch traced here: 90.9 us
  Pallas kernels  89.6 us (98%)
  between operations  1.29 us (1%)
    pallas_call x1, Pallas kernels, fused(): pl.pallas_call(functools.partial(kernel, sizes, rows, cols), out_shape=re...  57.1 us
    pallas_call x1, Pallas kernels, write_out(): pl.pallas_call(write_kernel, out_shape=tuple((jax.ShapeDtypeStruct(x.shap...  32.4 us

profile of v2, /device:TPU:0, one launch (start us, length us, event | category | flops | bytes accessed | tf_op | source)
XLA Modules:
  0.0 90.9 jit_solution(1038144631142039892)
XLA Ops:
  1.3 57.1 %shard_map.180 = (bf16[576,128]{1,0:T(8,128)(2,1)}, bf16[12,64,96]{2,1,0:T(8,128)(2,1)}, f32[576,128]{1,0:T(8,128)}, f32[128,256]{1,0:T(8,128)}, f32[128,256]{1,...) custom-call(s32[1,1]{1,0:T(1,128)} %bitcast.12.live_ref, bf16[576,128]{1,0:T(8,128)(2,1)} %bitcast.13, ...), custom_call_target="tpu_custom_call" | custom-call | tf_op jit(solution)/shard_map/pallas_call | solution.py:642
  58.4 32.4 %shard_map.181 = (bf16[576,128]{1,0:T(8,128)(2,1)}, bf16[12,64,96]{2,1,0:T(8,128)(2,1)}, f32[576,128]{1,0:T(8,128)}, f32[128,256]{1,0:T(8,128)}, f32[128,256]{1,...) custom-call(bf16[576,128]{1,0:T(8,128)(2,1)} %get-tuple-element.21.refs_0_, ...), custom_call_target="tpu_custom_call" | custom-call | tf_op jit(solution)/shard_map/pallas_call | solution.py:579

commit v3 on v2

--- a/solution.py
+++ b/solution.py
@@ -141,7 +141,7 @@
 
 most_vmem = (64 << 20) - (96 << 10)
 
-OPS, TRI, DTRI, DOPS, RS_A, AG_A, RS_B, AG_B, PHASES = range(9)
+OPS, TRI, DTRI, DOPS, RS_A, RS_B, AG_B, PHASES = range(8)
 
 
 def column_norm(field):
@@ -204,7 +204,7 @@
     ) = made
     (
     s_ops, r_ops, s_tri, r_tri, s_dtri, r_dtri, s_dops, r_dops,
-    s_rsa, r_rsa, s_aga, r_aga, s_rsb, r_rsb, s_agb, r_agb,
+    s_rsa, r_rsa, s_rsb, r_rsb, s_agb, r_agb,
     s_col, r_col,
     pair_buf, normed_buf, proj_buf, gate_buf, gout_buf, dlin_buf, dnew_buf, dgout_buf,
     pairs16, pairs8, left_buf, right_buf, flat16, flat8, cells_buf, rows_buf, col_f32, swap_f32,
@@ -433,7 +433,7 @@
             device_id_type=pl.DeviceIdType.MESH,
         )
 
-    for m in range(share):
+    for m in range(share // 2):
         for col in range(nch):
             slot = m * nch + col
             row = my_ch * share + m
@@ -470,6 +470,19 @@
             ]
         s_dops[q] = low(flat16[q])
     exchange(DOPS, s_dops, r_dops)
+    for m in range(share // 2, share):
+        for col in range(nch):
+            slot = m * nch + col
+            row = my_ch * share + m
+            here = row * nch + col == me
+
+            @pl.when(here)
+            def _():
+                r_col[my_row] = s_col[slot]
+
+            @pl.when(jnp.logical_not(here))
+            def _():
+                col_copy(slot, row, col).start()
 
     def summed(buf):
         total = wide(buf[0])
@@ -477,11 +490,39 @@
             total = total + wide(buf[q])
         return low(total)
 
+    d_normed_gout = matmul(w_gout_ref[...], dgout_buf[...])
+
+    arrive(DOPS, None, r_dops)
+    d_operands = jnp.concatenate(
+        [wide(r_dops[q])[0:per] for q in range(n)]
+        + [wide(r_dops[q])[per : 2 * per] for q in range(n)],
+        axis=0,
+    )
+    d_proj = low(d_operands * gate_buf[...])
+    d_gate = low(d_operands * proj_buf[...])
+    normed = normed_buf[...]
+    grad_proj = matmul(normed, d_proj, ((1,), (1,)))
+    grad_gate = matmul(normed, d_gate, ((1,), (1,)))
+    for q in range(n):
+        at = q * per
+        s_rsb[q] = low(
+            jnp.concatenate([grad_proj[at : at + per], grad_gate[at : at + per]], axis=0)
+        )
+    exchange(RS_B, s_rsb, r_rsb)
+
+    d_normed = d_normed_gout + matmul(w_proj_ref[...], d_proj) + matmul(w_gate_ref[...], d_gate)
+    unit_in, scale_in = column_norm(pair_buf[...])
+    d_pair = column_norm_back(unit_in, scale_in, d_normed * gain_in)
+    total = dnew_buf[...] + d_pair
+
+    arrive(RS_B, None, r_rsb)
     arrive(RS_A, None, r_rsa)
-    s_aga[...] = summed(r_rsa)
-    sent.extend(start(AG_A, lambda q: s_aga, r_aga))
-    r_aga[me] = s_aga[...]
-
+    s_agb[:, 0 : 2 * width] = summed(r_rsb)
+    s_agb[:, 2 * width : 3 * width] = summed(r_rsa)
+    sent.extend(start(AG_B, lambda q: s_agb, r_agb))
+    r_agb[me] = s_agb[...]
+    grad_ref[...] = total.T
+    store(2)
     for row in range(nblk * nsub):
         source = row * nch + my_row // share
 
@@ -503,52 +544,17 @@
     for j in range(rows):
         swapped_ref[j] = low(swap_f32[j].T)
     store(1)
-    d_normed_gout = matmul(w_gout_ref[...], dgout_buf[...])
-
-    arrive(DOPS, None, r_dops)
-    d_operands = jnp.concatenate(
-        [wide(r_dops[q])[0:per] for q in range(n)]
-        + [wide(r_dops[q])[per : 2 * per] for q in range(n)],
-        axis=0,
-    )
-    d_proj = low(d_operands * gate_buf[...])
-    d_gate = low(d_operands * proj_buf[...])
-    normed = normed_buf[...]
-    grad_proj = matmul(normed, d_proj, ((1,), (1,)))
-    grad_gate = matmul(normed, d_gate, ((1,), (1,)))
-    for q in range(n):
+    arrive(AG_B, None, r_agb)
+    for q in range(n):
+        x = wide(r_agb[q])
         at = q * per
-        s_rsb[q] = low(
-            jnp.concatenate([grad_proj[at : at + per], grad_gate[at : at + per]], axis=0)
-        )
-    exchange(RS_B, s_rsb, r_rsb)
-
-    d_normed = d_normed_gout + matmul(w_proj_ref[...], d_proj) + matmul(w_gate_ref[...], d_gate)
-    unit_in, scale_in = column_norm(pair_buf[...])
-    d_pair = column_norm_back(unit_in, scale_in, d_normed * gain_in)
-    total = dnew_buf[...] + d_pair
-
-    arrive(RS_B, None, r_rsb)
-    s_agb[...] = summed(r_rsb)
-    sent.extend(start(AG_B, lambda q: s_agb, r_agb))
-    r_agb[me] = s_agb[...]
-    grad_ref[...] = total.T
-    store(2)
-    arrive(AG_A, None, r_aga)
-    for q in range(n):
-        x = wide(r_aga[q])
-        g_gout_ref[q * per : (q + 1) * per, :] = x[0:per]
-        g_out_ref[q * per : (q + 1) * per, :] = x[per : 2 * per]
-    store(5)
-    store(6)
-    arrive(AG_B, None, r_agb)
-    for q in range(n):
-        x = wide(r_agb[q])
-        g_proj_ref[q * per : (q + 1) * per, :] = x[0:per]
-        g_gate_ref[q * per : (q + 1) * per, :] = x[per : 2 * per]
-
-    store(3)
-    store(4)
+        g_proj_ref[at : at + per, :] = x[0:per, 0 : 2 * width]
+        g_gate_ref[at : at + per, :] = x[per : 2 * per, 0 : 2 * width]
+        g_gout_ref[at : at + per, :] = x[0:per, 2 * width : 3 * width]
+        g_out_ref[at : at + per, :] = x[per : 2 * per, 2 * width : 3 * width]
+
+    for q in range(3, 7):
+        store(q)
     for copy in sent:
         copy.wait_send()
     for m in range(share):
@@ -564,24 +570,29 @@
         pltpu.make_async_copy(made[q], outputs[q], store_sem.at[q]).wait()
 
 
-def write_kernel(*refs):
-    count = len(refs) // 2
-    copies = [
-        pltpu.make_async_copy(refs[q], refs[count + q], refs[-1].at[q]) for q in range(count)
-    ]
-    for copy in copies:
+def write_kernel(count, *refs):
+    source, target, held = refs[:count], refs[count : 2 * count], refs[2 * count : 3 * count]
+    come, go = refs[3 * count :]
+    arriving = [pltpu.make_async_copy(source[q], held[q], come.at[q]) for q in range(count)]
+    leaving = [pltpu.make_async_copy(held[q], target[q], go.at[q]) for q in range(count)]
+    for copy in arriving:
         copy.start()
-    for copy in copies:
+    for one, other in zip(arriving, leaving):
+        one.wait()
+        other.start()
+    for copy in leaving:
         copy.wait()
 
 
 def write_out(values):
+    count = len(values)
     return pl.pallas_call(
-        write_kernel,
+        functools.partial(write_kernel, count),
         out_shape=tuple(jax.ShapeDtypeStruct(x.shape, x.dtype) for x in values),
-        in_specs=[pl.BlockSpec(memory_space=pltpu.HBM)] * len(values),
-        out_specs=[pl.BlockSpec(memory_space=pltpu.HBM)] * len(values),
-        scratch_shapes=[pltpu.SemaphoreType.DMA((len(values),))],
+        in_specs=[pl.BlockSpec(memory_space=pltpu.HBM)] * count,
+        out_specs=[pl.BlockSpec(memory_space=pltpu.HBM)] * count,
+        scratch_shapes=[pltpu.VMEM(x.shape, x.dtype) for x in values]
+        + [pltpu.SemaphoreType.DMA((count,))] * 2,
         compiler_params=pltpu.CompilerParams(vmem_limit_bytes=most_vmem),
     )(*values)
 
@@ -651,9 +662,8 @@
         + both(2 * per, half)
         + both(2 * per, cells)
         + both(2 * per, width)
-        + [vm((2 * per, width), bf), vm((n, 2 * per, width), bf)]
         + both(2 * per, 2 * width)
-        + [vm((2 * per, 2 * width), bf), vm((n, 2 * per, 2 * width), bf)]
+        + [vm((2 * per, 3 * width), bf), vm((n, 2 * per, 3 * width), bf)]
         + [vm((slots, col_rows, width), bf), vm((n // sizes["ch"], col_rows, width), bf)]
         + [
             vm((width, cells), f32),

time: 91 us -> 59.2 us (0.65)
  Pallas kernels: 89.6 us -> 57.8 us
    pallas_call x1, Pallas kernels: 32.4 us -> 2.09 us  [write_out(): pl.pallas_call(functools.partial(write_kernel, count), out_shape=tuple((j...]
    pallas_call x1, Pallas kernels: 57.1 us -> 55.7 us  [fused(): pl.pallas_call(functools.partial(kernel, sizes, rows, cols), out_shape=re...]
where the time goes in v3:
time: 59.2 us; the launch traced here: 59.1 us
  Pallas kernels  57.8 us (98%)
  between operations  1.29 us (2%)
    pallas_call x1, Pallas kernels, fused(): pl.pallas_call(functools.partial(kernel, sizes, rows, cols), out_shape=re...  55.7 us
    pallas_call x1, Pallas kernels, write_out(): pl.pallas_call(functools.partial(write_kernel, count), out_shape=tuple((j...  2.09 us

profile of v3, /device:TPU:0, one launch (start us, length us, event | category | flops | bytes accessed | tf_op | source)
XLA Modules:
  0.0 59.1 jit_solution(3031913017267301167)
XLA Ops:
  1.3 55.7 %shard_map.180 = (bf16[576,128]{1,0:T(8,128)(2,1)}, bf16[12,64,96]{2,1,0:T(8,128)(2,1)}, f32[576,128]{1,0:T(8,128)}, f32[128,256]{1,0:T(8,128)}, f32[128,256]{1,...) custom-call(s32[1,1]{1,0:T(1,128)} %bitcast.12.live_ref, bf16[576,128]{1,0:T(8,128)(2,1)} %bitcast.13, ...), custom_call_target="tpu_custom_call" | custom-call | tf_op jit(solution)/shard_map/pallas_call | solution.py:653
  57.0 2.1 %shard_map.181 = (bf16[576,128]{1,0:T(8,128)(2,1)}, bf16[12,64,96]{2,1,0:T(8,128)(2,1)}, f32[576,128]{1,0:T(8,128)}, f32[128,256]{1,0:T(8,128)}, f32[128,256]{1,...) custom-call(bf16[576,128]{1,0:T(8,128)(2,1)} %get-tuple-element.21.refs_0_, ...), custom_call_target="tpu_custom_call" | custom-call | tf_op jit(solution)/shard_map/pallas_call | solution.py:589

commit v4 on v3

--- a/solution.py
+++ b/solution.py
@@ -398,8 +398,9 @@
         )
     exchange(RS_A, s_rsa, r_rsa)
 
-    rows_buf[...] = (pair_buf[...] + moved).T
-    new_ref[...] = low(rows_buf[...])
+    new_rows = (pair_buf[...] + moved).T
+    rows_buf[0:cells, :] = new_rows
+    new_ref[...] = low(new_rows)
     store(0)
     share = cols // rows
     lanes = width // nch
@@ -681,7 +682,7 @@
             vm((n, 2 * per, cells), f32),
             vm((n, 2 * per, half), f32),
             vm((width, cells), f32),
-            vm((cells, width), f32),
+            vm((-(-rows // 8) * 8 * cols, width), f32),
             vm((slots, col_rows, width), f32),
             vm((rows, tokens, lanes), f32),
             pltpu.SemaphoreType.DMA((PHASES, n)),

time: 59.2 us -> 59.2 us (level)
  no operation moved by 1% of the time
where the time goes in v4:
time: 59.2 us; the launch traced here: 59.1 us
  Pallas kernels  57.8 us (98%)
  between operations  1.29 us (2%)
    pallas_call x1, Pallas kernels, fused(): pl.pallas_call(functools.partial(kernel, sizes, rows, cols), out_shape=re...  55.7 us
    pallas_call x1, Pallas kernels, write_out(): pl.pallas_call(functools.partial(write_kernel, count), out_shape=tuple((j...  2.09 us

profile of v4, /device:TPU:0, one launch (start us, length us, event | category | flops | bytes accessed | tf_op | source)
XLA Modules:
  0.0 59.1 jit_solution(15068929753875764998)
XLA Ops:
  1.3 55.7 %shard_map.180 = (bf16[576,128]{1,0:T(8,128)(2,1)}, bf16[12,64,96]{2,1,0:T(8,128)(2,1)}, f32[576,128]{1,0:T(8,128)}, f32[128,256]{1,0:T(8,128)}, f32[128,256]{1,...) custom-call(s32[1,1]{1,0:T(1,128)} %bitcast.12.live_ref, bf16[576,128]{1,0:T(8,128)(2,1)} %bitcast.13, ...), custom_call_target="tpu_custom_call" | custom-call | tf_op jit(solution)/shard_map/pallas_call | solution.py:654
  57.0 2.1 %shard_map.181 = (bf16[576,128]{1,0:T(8,128)(2,1)}, bf16[12,64,96]{2,1,0:T(8,128)(2,1)}, f32[576,128]{1,0:T(8,128)}, f32[128,256]{1,0:T(8,128)}, f32[128,256]{1,...) custom-call(bf16[576,128]{1,0:T(8,128)(2,1)} %get-tuple-element.21.refs_0_, ...), custom_call_target="tpu_custom_call" | custom-call | tf_op jit(solution)/shard_map/pallas_call | solution.py:590
